TPU v7x, 32 devices: a whole 2x2x4 slice. The times are simulated.
32 devices in a mesh: pts: 16 (over z, x, core), dir: 2 (over y).
Axes of the slice: x: 2, y: 2, z: 4, core: 2. Of those that a mesh axis runs over, the one named last changes fastest.
Arguments:
- action: float32 [50, 32, 256, 256], P(None, 'dir', 'pts'), may hold values from 0 to 60, as said below
- currents: float32 [2, 256, 256], P(None, 'pts'), may hold values from -0.1 to 0.1, as said below
- land_mask: int32 [256, 256], P('pts'), may hold values 0 or 1
- group_speed: float32 [50], replicated, may hold values from 0.02 to 0.55
- group_ratio: float32 [50], replicated, may hold values from 0.5 to 1
- bin_weight: float32 [50], replicated, may hold values from 0.002 to 0.02
Outputs:
- new_action: float32 [50, 32, 256, 256], P(None, 'dir', 'pts')
- wave_force: float32 [2, 256, 256], P(None, 'pts')
Inputs may be any that keep to these rules, and one draw needn't show every extreme that they name: Positive action densities. currents vary slowly from point to point.
All inputs are finite; a program needn't handle non-finite values. No bound on the sum of `land_mask` on one device may be relied on, other than what follows from the above.
Results may differ from a plain program's by a relative error of at most 0.00022.
Values sent between devices are 32-bit elements; how exact they have to be, the bound alone decides.
A program may use at most 128 MiB of HBM per device.

v0:
```python
import functools
import math

import jax
import jax.numpy as jnp
from jax import lax
from jax.experimental import pallas as pl
from jax.experimental.pallas import tpu as pltpu
from jax.sharding import PartitionSpec as P

MESH = pl.DeviceIdType.MESH
LANES = 128
SUBS = 8
F32 = jnp.float32


def lane_of(shape):
    return lax.broadcasted_iota(jnp.int32, shape, 1)


def next_col(tiles):
    count = len(tiles)
    edge = lane_of(tiles[0].shape) == LANES - 1
    rolled = [pltpu.roll(t, LANES - 1, 1) for t in tiles]
    return [
        jnp.where(edge, rolled[c + 1] if c + 1 < count else 0.0, rolled[c])
        for c in range(count)
    ]


def prev_col(tiles, first):
    edge = lane_of(tiles[0].shape) == 0
    rolled = [pltpu.roll(t, 1, 1) for t in tiles]
    return [jnp.where(edge, rolled[c - 1] if c else first, rolled[c]) for c in range(len(tiles))]


def next_row(tiles, below):
    count = len(tiles)
    edge = lax.broadcasted_iota(jnp.int32, (SUBS, LANES), 0) == SUBS - 1
    rolled = [[pltpu.roll(t, SUBS - 1, 0) for t in row] for row in tiles]
    return [
        [
            jnp.where(edge, rolled[r + 1][c] if r + 1 < count else below[c], rolled[r][c])
            for c in range(len(below))
        ]
        for r in range(count)
    ]


def prev_row(tiles, above):
    edge = lax.broadcasted_iota(jnp.int32, (SUBS, LANES), 0) == 0
    rolled = [[pltpu.roll(t, 1, 0) for t in row] for row in tiles]
    return [
        [jnp.where(edge, rolled[r - 1][c] if r else above[c], rolled[r][c]) for c in range(len(above))]
        for r in range(len(tiles))
    ]


def split_cols(value):
    return [value[:, c * LANES:(c + 1) * LANES] for c in range(value.shape[1] // LANES)]


def load_tiles(ref, *lead):
    rows, cols = ref.shape[-2:]
    return [
        [
            ref[(*lead, pl.ds(r * SUBS, SUBS), pl.ds(c * LANES, LANES))]
            for c in range(cols // LANES)
        ]
        for r in range(rows // SUBS)
    ]


def load_row(ref, *lead):
    cols = ref.shape[-1]
    *head, row = lead
    return [ref[(*head, pl.ds(row, 1), pl.ds(c * LANES, LANES))] for c in range(cols // LANES)]


def store_tiles(ref, tiles, *lead):
    for r, row in enumerate(tiles):
        for c, tile in enumerate(row):
            ref[(*lead, pl.ds(r * SUBS, SUBS), pl.ds(c * LANES, LANES))] = tile


def pick(speed, behind, ahead):
    return speed * jnp.where(speed > 0.0, behind, ahead)


def transport_kernel(
    n_pts, n_dir, chunk,
    act, cur, land, gs, trig, cosb, sinb, face,
    a2, got, k_ref,
    buf, own_top, own_bot, halo_top, halo_bot, cur_top, cur_bot, land_top, land_bot,
    ub, vb, sea, rows, border, sel,
    in_sem, out_sem, up_send, up_recv, down_send, down_recv, cur_sem, dir_send, dir_recv,
):
    nf, nd, nr, nc = buf.shape
    chunks = nf // chunk
    ct = nc // LANES
    me = lax.axis_index("pts")
    mine = lax.axis_index("dir")
    has_prev = me > 0
    has_next = me < n_pts - 1
    before = jnp.maximum(me - 1, 0)
    after = jnp.minimum(me + 1, n_pts - 1)
    dir_after = lax.rem(mine + 1, n_dir)
    dir_before = lax.rem(mine + n_dir - 1, n_dir)

    def bring(c):
        part = pl.ds(c * chunk, chunk)
        return pltpu.make_async_copy(act.at[part], buf.at[part], in_sem.at[c])

    def put(c):
        part = pl.ds(c * chunk, chunk)
        return pltpu.make_async_copy(buf.at[part], a2.at[part], out_sem.at[c])

    def remote(src, dst, send, recv, where):
        return pltpu.make_async_remote_copy(
            src_ref=src, dst_ref=dst, send_sem=send, recv_sem=recv,
            device_id=where, device_id_type=MESH,
        )

    def up(c):
        part = pl.ds(c * chunk, chunk)
        return remote(own_top.at[part], halo_bot.at[part], up_send.at[c], up_recv.at[c], {"pts": before})

    def down(c):
        part = pl.ds(c * chunk, chunk)
        return remote(own_bot.at[part], halo_top.at[part], down_send.at[c], down_recv.at[c], {"pts": after})

    def cur_up():
        return remote(cur.at[:, pl.ds(0, SUBS)], cur_bot, cur_sem.at[0], cur_sem.at[1], {"pts": before})

    def cur_down():
        return remote(cur.at[:, pl.ds(nr - SUBS, SUBS)], cur_top, cur_sem.at[2], cur_sem.at[3], {"pts": after})

    def land_up():
        return remote(land.at[pl.ds(0, SUBS)], land_bot, cur_sem.at[4], cur_sem.at[5], {"pts": before})

    def land_down():
        return remote(land.at[pl.ds(nr - SUBS, SUBS)], land_top, cur_sem.at[6], cur_sem.at[7], {"pts": after})

    def turn(side, c):
        part = pl.ds(c * chunk, chunk)
        return remote(
            sel.at[side, part], got.at[side, part], dir_send.at[side, c], dir_recv.at[side, c],
            {"dir": dir_after if side == 0 else dir_before},
        )

    sides = sel.shape[0]

    def start_in(c, _):
        bring(c).start()
        return 0

    lax.fori_loop(0, chunks, start_in, 0)

    barrier = pltpu.get_barrier_semaphore()

    @pl.when(has_prev)
    def _():
        pl.semaphore_signal(barrier, inc=1, device_id={"pts": before}, device_id_type=MESH)

    @pl.when(has_next)
    def _():
        pl.semaphore_signal(barrier, inc=1, device_id={"pts": after}, device_id_type=MESH)

    pl.semaphore_signal(barrier, inc=1, device_id={"dir": dir_after}, device_id_type=MESH)
    if n_dir > 2:
        pl.semaphore_signal(barrier, inc=1, device_id={"dir": dir_before}, device_id_type=MESH)

    @pl.when(jnp.logical_not(has_prev))
    def _():
        def clear(f, _):
            halo_top[f] = jnp.zeros(halo_top.shape[1:], F32)
            return 0
        lax.fori_loop(0, nf, clear, 0)
        cur_top[...] = jnp.zeros(cur_top.shape, F32)
        land_top[...] = jnp.zeros(land_top.shape, jnp.int32)

    @pl.when(jnp.logical_not(has_next))
    def _():
        def clear(f, _):
            halo_bot[f] = jnp.zeros(halo_bot.shape[1:], F32)
            return 0
        lax.fori_loop(0, nf, clear, 0)
        cur_bot[...] = jnp.zeros(cur_bot.shape, F32)
        land_bot[...] = jnp.zeros(land_bot.shape, jnp.int32)

    others = has_prev.astype(jnp.int32) + has_next.astype(jnp.int32)
    pl.semaphore_wait(barrier, others + (2 if n_dir > 2 else 1))

    @pl.when(has_prev)
    def _():
        cur_up().start()
        land_up().start()

    @pl.when(has_next)
    def _():
        cur_down().start()
        land_down().start()

    def pack_chunk(c, _):
        bring(c).wait()

        def pack(i, _):
            f = c * chunk + i
            for d in range(nd):
                for w in range(2):
                    own_top[f, w, pl.ds(d, 1), :] = buf[f, d, pl.ds(w, 1), :]
                    own_bot[f, w, pl.ds(d, 1), :] = buf[f, d, pl.ds(nr - 2 + w, 1), :]
            return 0

        lax.fori_loop(0, chunk, pack, 0)

        @pl.when(has_prev)
        def _():
            up(c).start()

        @pl.when(has_next)
        def _():
            down(c).start()

        return 0

    lax.fori_loop(0, chunks, pack_chunk, 0)

    @pl.when(has_prev)
    def _():
        cur_down().wait_recv()
        land_down().wait_recv()

    @pl.when(has_next)
    def _():
        cur_up().wait_recv()
        land_up().wait_recv()

    u, v = load_tiles(cur, 0), load_tiles(cur, 1)
    rt = len(u)
    u_next = next_row(u, load_row(cur_bot, 0, 0))
    u_prev = prev_row(u, load_row(cur_top, 0, SUBS - 1))
    v_next = next_row(v, load_row(cur_bot, 1, 0))
    v_prev = prev_row(v, load_row(cur_top, 1, SUBS - 1))
    store_tiles(ub, [[0.5 * (u[r][c] + u_next[r][c]) for c in range(ct)] for r in range(rt)])
    sea[...] = land[...].astype(F32)
    for r in range(rt):
        u_east, v_east = next_col(u[r]), next_col(v[r])
        u_west, v_west = prev_col(u[r], 0.0), prev_col(v[r], 0.0)
        for c in range(ct):
            at = (pl.ds(r * SUBS, SUBS), pl.ds(c * LANES, LANES))
            vb[at] = 0.5 * (v[r][c] + v_east[c])
            u_dx = 0.5 * (u_next[r][c] - u_prev[r][c])
            v_dx = 0.5 * (v_next[r][c] - v_prev[r][c])
            u_dy = 0.5 * (u_east[c] - u_west[c])
            v_dy = 0.5 * (v_east[c] - v_west[c])
            for d in range(nd + 1):
                k_ref[(d, *at)] = face[0, d] * (u_dx - v_dy) + face[1, d] * u_dy - face[2, d] * v_dx

    def mean(x, y):
        return [0.5 * (p + q) for p, q in zip(x, y)]

    u_rows = [
        load_row(cur_top, 0, SUBS - 2), load_row(cur_top, 0, SUBS - 1), load_row(cur, 0, 0),
        load_row(cur, 0, 1), load_row(cur, 0, nr - 1), load_row(cur_bot, 0, 0), load_row(cur_bot, 0, 1),
    ]
    v_rows = [load_row(cur_top, 1, SUBS - 1), load_row(cur, 1, 0), load_row(cur_bot, 1, 0)]
    kept = [mean(u_rows[i], u_rows[i + 1]) for i in (0, 1, 2, 4, 5)]
    kept += [mean(x, next_col(x)) for x in v_rows]
    kept += [[0.5 * t for t in x] for x in v_rows]
    kept += [
        [t.astype(F32) for t in x]
        for x in (
            load_row(land_top, SUBS - 2), load_row(land_top, SUBS - 1), load_row(land, 0),
            load_row(land, 1), load_row(land, nr - 1), load_row(land_bot, 0), load_row(land_bot, 1),
        )
    ]
    for i, tiles in enumerate(kept):
        for c in range(ct):
            rows[pl.ds(i, 1), pl.ds(c * LANES, LANES)] = tiles[c]

    def edge_step(a, into, out, speed_y, which, land_row):
        v_face, v_half = load_row(rows, 5 + which), load_row(rows, 8 + which)
        east = next_col(a)
        flux = [pick(speed_y[c] + v_face[c], a[c], east[c]) for c in range(ct)]
        west = prev_col(flux, jnp.minimum(speed_y[0] + v_half[0], 0.0) * a[0])
        return [
            land_row[c] * (a[c] - ((out[c] - into[c]) + (flux[c] - west[c]))) for c in range(ct)
        ]

    def edges(f):
        speed_x = [gs[f] * t for t in split_cols(cosb[...])]
        speed_y = [gs[f] * t for t in split_cols(sinb[...])]
        lands = [load_row(rows, 11 + i) for i in range(7)]

        def cells(ref, w, i):
            return [lands[i][c] * t for c, t in enumerate(split_cols(ref[f, w]))]

        def across(i, behind, ahead):
            u_face = load_row(rows, i)
            return [pick(speed_x[c] + u_face[c], behind[c], ahead[c]) for c in range(ct)]

        p2, p1 = cells(halo_top, 0, 0), cells(halo_top, 1, 1)
        a0, a1 = cells(own_top, 0, 2), cells(own_top, 1, 3)
        f_far, f_top, f_in = across(0, p2, p1), across(1, p1, a0), across(2, a0, a1)
        above = edge_step(p1, f_far, f_top, speed_y, 0, lands[1])
        first = edge_step(a0, f_top, f_in, speed_y, 1, lands[2])
        f_top2 = across(1, above, first)
        last = cells(own_bot, 1, 4)
        n0, n1 = cells(halo_bot, 0, 5), cells(halo_bot, 1, 6)
        below = edge_step(n0, across(3, last, n0), across(4, n0, n1), speed_y, 2, lands[5])
        for i, tiles in enumerate((f_top, f_top2, n0, below)):
            for c in range(ct):
                border[i, :, pl.ds(c * LANES, LANES)] = tiles[c]

    def one(f, d):
        speed_x, speed_y = gs[f] * trig[0, d], gs[f] * trig[1, d]
        lands = load_tiles(sea)
        cx = [[speed_x + t for t in row] for row in load_tiles(ub)]
        cy = [[speed_y + t for t in row] for row in load_tiles(vb)]
        out_west = [
            jnp.minimum(speed_y + 0.5 * cur[1, pl.ds(r * SUBS, SUBS), pl.ds(0, LANES)], 0.0)
            for r in range(rt)
        ]
        a = load_tiles(buf, f, d)
        a = [[lands[r][c] * a[r][c] for c in range(ct)] for r in range(rt)]
        for step in range(2):
            south = next_row(a, load_row(border, 2 + step, d))
            fx = [[pick(cx[r][c], a[r][c], south[r][c]) for c in range(ct)] for r in range(rt)]
            fx_prev = prev_row(fx, load_row(border, step, d))
            new = []
            for r in range(rt):
                east = next_col(a[r])
                fy = [pick(cy[r][c], a[r][c], east[c]) for c in range(ct)]
                fy_prev = prev_col(fy, out_west[r] * a[r][0])
                new.append([
                    lands[r][c] * (a[r][c] - ((fx[r][c] - fx_prev[r][c]) + (fy[c] - fy_prev[c])))
                    for c in range(ct)
                ])
            a = new
        store_tiles(buf, a, f, d)

    def work_chunk(c, _):
        @pl.when(has_prev)
        def _():
            down(c).wait_recv()

        @pl.when(has_next)
        def _():
            up(c).wait_recv()

        def work(i, _):
            f = c * chunk + i
            edges(f)

            for d in range(nd):
                one(f, d)
            if sides == 1:
                sel[0, f] = jnp.where(k_ref[0] > 0.0, buf[f, nd - 1], buf[f, 0])
            else:
                sel[0, f] = buf[f, nd - 1]
                sel[1, f] = buf[f, 0]
            return 0

        lax.fori_loop(0, chunk, work, 0)
        put(c).start()
        for side in range(sides):
            turn(side, c).start()
        return 0

    lax.fori_loop(0, chunks, work_chunk, 0)

    def finish(c, _):
        put(c).wait()
        for side in range(sides):
            turn(side, c).wait()

        @pl.when(has_prev)
        def _():
            up(c).wait_send()

        @pl.when(has_next)
        def _():
            down(c).wait_send()

        return 0

    lax.fori_loop(0, chunks, finish, 0)

    @pl.when(has_prev)
    def _():
        cur_up().wait_send()
        land_up().wait_send()

    @pl.when(has_next)
    def _():
        cur_down().wait_send()
        land_down().wait_send()


def refract_kernel(a2, got, k_ref, table, weight, new, stress):
    nf, nd, nr, nc = a2.shape
    step = pl.program_id(0)

    @pl.when(step == 0)
    def _():
        stress[...] = jnp.zeros(stress.shape, F32)

    def work(i, _):
        f = step * nf + i
        for r in range(nr // SUBS):
            for c in range(nc // LANES):
                at = (pl.ds(r * SUBS, SUBS), pl.ds(c * LANES, LANES))
                here = a2[(i, 0, *at)]
                flux = pick(k_ref[(0, *at)], got[(0, i, *at)], here)
                total = even = odd = None
                for d in range(nd):
                    ahead = a2[(i, d + 1, *at)] if d + 1 < nd else got[(got.shape[0] - 1, i, *at)]
                    after = pick(k_ref[(d + 1, *at)], here, ahead)
                    value = here - (after - flux)
                    new[(i, d, *at)] = value
                    p, q = table[0, d] * value, table[1, d] * value
                    total = value if d == 0 else total + value
                    even = p if d == 0 else even + p
                    odd = q if d == 0 else odd + q
                    here, flux = ahead, after
                w, wr = weight[0, f], weight[1, f]
                half = (0.5 * w) * total
                stress[(0, *at)] += wr * (total + even) - half
                stress[(1, *at)] += wr * odd
                stress[(2, *at)] += wr * ((total + total) - even) - half
        return 0

    lax.fori_loop(0, nf, work, 0)


def with_rows(value, axis):
    count, length = lax.axis_size(axis), value.shape[1]
    up = [(i, i + 1) for i in range(count - 1)]
    before = lax.ppermute(value[:, length - 1:], axis, up)
    after = lax.ppermute(value[:, :1], axis, [(j, i) for i, j in up])
    return jnp.concatenate([before, value, after], axis=1)


def col_slope(values):
    padded = jnp.pad(values[1:-1], ((0, 0), (1, 1)))
    return 0.5 * (padded[:, 2:] - padded[:, :-2])


def row_slope(values):
    return 0.5 * (values[2:] - values[:-2])


def per_device(action, currents, land_mask, group_speed, group_ratio, bin_weight):
    nf, nd, nr, nc = action.shape
    n_pts, n_dir = lax.axis_size("pts"), lax.axis_size("dir")
    total_dirs = nd * n_dir
    step_angle = 2.0 * math.pi / total_dirs
    offset = lax.axis_index("dir") * nd
    angles = (offset + jnp.arange(nd)).astype(F32) * step_angle
    trig = jnp.stack([jnp.cos(angles), jnp.sin(angles)])
    face_offset = 0 if n_dir == 2 else offset
    face_index = jnp.arange(nd + 1)
    if n_dir == 2:
        face_index = face_index % nd
    face_angles = ((face_offset + face_index).astype(F32) - 0.5) * step_angle
    scale = total_dirs / (2.0 * math.pi)
    fs, fc = jnp.sin(face_angles), jnp.cos(face_angles)
    face = scale * jnp.stack([fs * fc, fs * fs, fc * fc])
    cosb = jnp.broadcast_to(trig[0][:, None], (nd, nc))
    sinb = jnp.broadcast_to(trig[1][:, None], (nd, nc))
    chunk = max(c for c in range(1, 6) if nf % c == 0)
    chunks = nf // chunk
    sides = 1 if n_dir == 2 else 2
    vmem = pl.BlockSpec(memory_space=pltpu.VMEM)
    smem = pl.BlockSpec(memory_space=pltpu.SMEM)
    hbm = pl.BlockSpec(memory_space=pl.ANY)
    dma = pltpu.SemaphoreType.DMA
    halo = pltpu.VMEM((nf, 2, nd, nc), F32)
    a2, got, turning = pl.pallas_call(
        functools.partial(transport_kernel, n_pts, n_dir, chunk),
        out_shape=(
            jax.ShapeDtypeStruct(action.shape, F32),
            jax.ShapeDtypeStruct((sides, nf, nr, nc), F32),
            jax.ShapeDtypeStruct((nd + 1, nr, nc), F32),
        ),
        in_specs=[hbm, vmem, vmem, smem, smem, vmem, vmem, smem],
        out_specs=(hbm, hbm, vmem),
        scratch_shapes=[
            pltpu.VMEM(action.shape, F32), halo, halo, halo, halo,
            pltpu.VMEM((2, SUBS, nc), F32), pltpu.VMEM((2, SUBS, nc), F32),
            pltpu.VMEM((SUBS, nc), jnp.int32), pltpu.VMEM((SUBS, nc), jnp.int32),
            pltpu.VMEM((nr, nc), F32), pltpu.VMEM((nr, nc), F32), pltpu.VMEM((nr, nc), F32),
            pltpu.VMEM((24, nc), F32), pltpu.VMEM((4, nd, nc), F32),
            pltpu.VMEM((sides, nf, nr, nc), F32),
            dma((chunks,)), dma((chunks,)), dma((chunks,)), dma((chunks,)), dma((chunks,)),
            dma((chunks,)), dma((8,)), dma((sides, chunks)), dma((sides, chunks)),
        ],
        compiler_params=pltpu.CompilerParams(
            collective_id=0, has_side_effects=True, vmem_limit_bytes=40 * 2**20
        ),
        name="transport",
    )(action, currents, land_mask, group_speed, trig, cosb, sinb, face)
    table = jnp.stack([trig[0] * trig[0], trig[0] * trig[1]])
    weight = jnp.stack([bin_weight, bin_weight * group_ratio])
    new_action, stress = pl.pallas_call(
        refract_kernel,
        grid=(chunks,),
        out_shape=(
            jax.ShapeDtypeStruct(action.shape, F32),
            jax.ShapeDtypeStruct((3, nr, nc), F32),
        ),
        in_specs=[
            pl.BlockSpec((chunk, nd, nr, nc), lambda i: (i, 0, 0, 0)),
            pl.BlockSpec((sides, chunk, nr, nc), lambda i: (0, i, 0, 0)),
            pl.BlockSpec((nd + 1, nr, nc), lambda i: (0, 0, 0)),
            smem, smem,
        ],
        out_specs=(
            pl.BlockSpec((chunk, nd, nr, nc), lambda i: (i, 0, 0, 0)),
            pl.BlockSpec((3, nr, nc), lambda i: (0, 0, 0)),
        ),
        compiler_params=pltpu.CompilerParams(vmem_limit_bytes=40 * 2**20),
        name="refract",
    )(a2, got, turning, table, weight)
    ext = lax.psum(with_rows(stress, "pts"), "dir")
    first = -(row_slope(ext[0]) + col_slope(ext[1]))
    second = -(row_slope(ext[1]) + col_slope(ext[2]))
    return new_action, jnp.stack([first, second])


def solution(mesh):
    in_specs = (P(None, "dir", "pts", None), P(None, "pts", None), P("pts", None), P(), P(), P())
    out_specs = (P(None, "dir", "pts", None), P(None, "pts", None))
    return jax.shard_map(
        per_device, mesh=mesh, in_specs=in_specs, out_specs=out_specs, check_vma=False
    )
```

profile of v0, /device:TPU:0, one launch (start us, length us, event | category | flops | bytes accessed | tf_op | source)
XLA Modules:
  0.0 100.9 jit_solution(2287847573628606198)
XLA Ops:
  0.9 0.7 multiply_bitcast_fusion
  1.6 0.7 pad_maximum_fusion.4.weight
  2.3 0.1 broadcast_in_dim.5.sinb
  2.3 0.1 broadcast_in_dim.4.cosb
  2.4 0.0 copy-start.2
  2.4 0.8 copy-done.2
  3.2 0.0 copy-start.3
  3.2 0.7 copy-done.3
  3.9 0.0 copy-start.4
  3.9 0.7 copy-done.4
  4.5 45.5 %transport.1 = (f32[50,16,16,256]{3,2,1,0:T(8,128)S(1)}, f32[1,50,16,256]{3,2,1,0:T(8,128)S(1)}, f32[17,16,256]{2,1,0:T(8,128)S(1)}) custom-call(f32[50,16,16,256]{3,2,1,0:T(8,128)} %act.1, f32[2,16,256]{2,1,0:T(8,128)S(1)} %copy-done.2, s32[16,256]{1,0:T(8,128)S(1)} %copy-done.3, f32[50]{0:T(128)S(1)} %copy-done.4, f32[2,16]{1,0:T(2,128)S(1)} %pad_maximum_fusion.2.trig, ...), custom_call_target="tpu_custom_call" | custom-call | tf_op jit(solution)/shard_map/transport/pallas_call | solution.py:480
  50.1 0.0 copy-start
  50.1 4.9 %copy-done = f32[50,16,16,256]{3,2,1,0:T(8,128)} copy-done((f32[50,16,16,256]{3,2,1,0:T(8,128)}, f32[50,16,16,256]{3,2,1,0:T(8,128)S(1)}, u32[]{:S(2)}) %copy-start) | copy-done | bytes 13107224
  55.0 0.0 copy-start.1
  55.0 4.7 %copy-done.1 = f32[50,16,16,256]{3,2,1,0:T(8,128)S(1)} copy-done((f32[50,16,16,256]{3,2,1,0:T(8,128)S(1)}, f32[50,16,16,256]{3,2,1,0:T(8,128)}, u32[]{:S(2)}) %copy-start.1) | copy-done | bytes 13107224
  59.7 9.2 %refract.1 = (f32[50,16,16,256]{3,2,1,0:T(8,128)}, f32[3,16,256]{2,1,0:T(8,128)S(1)}) custom-call(f32[50,16,16,256]{3,2,1,0:T(8,128)S(1)} %copy-done.1, f32[1,50,16,256]{3,2,1,0:T(8,128)S(1)} %get-tuple-element.8.got, f32[17,16,256]{2,1,0:T(8,128)S(1)} %get-tuple-element.9.k_ref, f32[2,16]{1,0:T(2,128)S(1)} %pad_maximum_fusion.3.table, ...), custom_call_target="tpu_custom_call" | custom-call | tf_op jit(solution)/shard_map/refract/pallas_call | solution.py:506
  69.0 2.0 %collective-permute-start = (f32[3,1,256]{2,1,0:T(1,128)S(1)}, f32[3,1,256]{2,1,0:T(1,128)S(1)}, u32[]{:S(2)}, u32[]{:S(2)}) collective-permute-start(f32[3,1,256]{2,1,0:T(1,128)S(1)} %get-tuple-element.16), channel_id=1, source_target_pairs={{0,2},{2,4},{4,6},{6,8},{8,10},{10,12},{12,14},{14,16},{16,18},{18... | collective-permute-start | bytes 9224 | tf_op jit(solution)/shard_map/ppermute | solution.py:440
  71.0 1.3 %collective-permute-start.1 = (f32[3,1,256]{2,1,0:T(1,128)S(1)}, f32[3,1,256]{2,1,0:T(1,128)S(1)}, u32[]{:S(2)}, u32[]{:S(2)}) collective-permute-start(f32[3,1,256]{2,1,0:T(1,128)S(1)} %get-tuple-element.17), channel_id=1, source_target_pairs={{2,0},{4,2},{6,4},{8,6},{10,8},{12,10},{14,12},{16,14},{18,16},{20... | collective-permute-start | bytes 9224 | tf_op jit(solution)/shard_map/ppermute | solution.py:441
  72.3 0.0 collective-permute-done
  72.3 19.9 %collective-permute-done.1 = f32[3,1,256]{2,1,0:T(1,128)S(1)} collective-permute-done((f32[3,1,256]{2,1,0:T(1,128)S(1)}, f32[3,1,256]{2,1,0:T(1,128)S(1)}, u32[]{:S(2)}, u32[]{:S(2)}) %collective-permute-start.1) | collective-permute-done | bytes 3104 | tf_op jit(solution)/shard_map/ppermute | solution.py:441
  92.3 7.8 %psum.7 = f32[3,18,256]{2,1,0:T(8,128)S(1)} all-reduce(f32[3,18,256]{2,1,0:T(8,128)S(1)} %pad_maximum_fusion), channel_id=1, replica_groups=mesh['pts'=16,'dir'=2] {'dir'}, use_global_device_ids=true, to_apply=%region_0.1 | all-reduce | flops 13824 | bytes 110592 | tf_op jit(solution)/shard_map/psum | solution.py:526
  100.1 0.1 fusion.4
  100.2 0.6 pad_maximum_fusion.1
  (11 shorter events, 0.3 us)
Async XLA Ops:
  2.4 0.8 copy-start.2
  3.2 0.7 copy-start.3
  3.9 0.7 copy-start.4
  50.1 5.0 %copy-start = (f32[50,16,16,256]{3,2,1,0:T(8,128)}, f32[50,16,16,256]{3,2,1,0:T(8,128)S(1)}, u32[]{:S(2)}) copy-start(f32[50,16,16,256]{3,2,1,0:T(8,128)S(1)} %get-tuple-element.7.a2) | copy-start | bytes 39321604
  55.0 4.7 %copy-start.1 = (f32[50,16,16,256]{3,2,1,0:T(8,128)S(1)}, f32[50,16,16,256]{3,2,1,0:T(8,128)}, u32[]{:S(2)}) copy-start(f32[50,16,16,256]{3,2,1,0:T(8,128)} %copy-done) | copy-start | bytes 39321604
  69.0 3.3 %collective-permute-start = (f32[3,1,256]{2,1,0:T(1,128)S(1)}, f32[3,1,256]{2,1,0:T(1,128)S(1)}, u32[]{:S(2)}, u32[]{:S(2)}) collective-permute-start(f32[3,1,256]{2,1,0:T(1,128)S(1)} %get-tuple-element.16), channel_id=1, source_target_pairs={{0,2},{2,4},{4,6},{6,8},{8,10},{10,12},{12,14},{14,16},{16,18},{18... | collective-permute-start | bytes 9224 | tf_op jit(solution)/shard_map/ppermute | solution.py:440
  71.0 21.2 %collective-permute-start.1 = (f32[3,1,256]{2,1,0:T(1,128)S(1)}, f32[3,1,256]{2,1,0:T(1,128)S(1)}, u32[]{:S(2)}, u32[]{:S(2)}) collective-permute-start(f32[3,1,256]{2,1,0:T(1,128)S(1)} %get-tuple-element.17), channel_id=1, source_target_pairs={{2,0},{4,2},{6,4},{8,6},{10,8},{12,10},{14,12},{16,14},{18,16},{20... | collective-permute-start | bytes 9224 | tf_op jit(solution)/shard_map/ppermute | solution.py:441
where the time goes:
time: 101 us
  Pallas kernels  54.7 us (54%)
  waiting for transfers between devices  19.9 us (20%)
  local copies, waits for them, and re-layouts  12 us (12%)
  blocking collectives  7.83 us (8%)
  starting transfers between devices  3.33 us (3%)
  other arithmetic  2.32 us (2%)
    pallas_call x1, Pallas kernels, per_device(): pl.pallas_call(functools.partial(transport_kernel, n_pts, n_dir, chunk),...  45.5 us
    ppermute x1, waiting for transfers between devices, with_rows(): after = lax.ppermute(value[:, :1], axis, [(j, i) for i, j in up])  19.9 us
    unnamed x10, local copies, waits for them, and re-layouts  11.8 us
    pallas_call x1, Pallas kernels, per_device(): pl.pallas_call(refract_kernel, grid=(chunks,), out_shape=(jax.ShapeDtypeS...  9.23 us
    psum x1, blocking collectives, per_device(): ext = lax.psum(with_rows(stress, 'pts'), 'dir')  7.83 us
    ppermute x1, starting transfers between devices, with_rows(): before = lax.ppermute(value[:, length - 1:], axis, up)  2.04 us
  transfers between devices with their start and end apart: 2, of which 1 were waited for; matrix products, arithmetic and copies ran while one was open for 0% of the time, Pallas kernels for 0%

commit v1 on v0

--- a/solution.py
+++ b/solution.py
@@ -3,6 +3,7 @@
 
 import jax
 import jax.numpy as jnp
+import numpy as np
 from jax import lax
 from jax.experimental import pallas as pl
 from jax.experimental.pallas import tpu as pltpu
@@ -89,11 +90,11 @@
 
 def transport_kernel(
     n_pts, n_dir, chunk,
-    act, cur, land, gs, trig, cosb, sinb, face,
-    a2, got, k_ref,
-    buf, own_top, own_bot, halo_top, halo_bot, cur_top, cur_bot, land_top, land_bot,
+    act, cur, land, gs, weight, table, wave,
+    buf, stress,
+    got, k_ref, own_top, own_bot, halo_top, halo_bot, cur_top, cur_bot, land_top, land_bot,
     ub, vb, sea, rows, border, sel,
-    in_sem, out_sem, up_send, up_recv, down_send, down_recv, cur_sem, dir_send, dir_recv,
+    in_sem, up_send, up_recv, down_send, down_recv, cur_sem, dir_send, dir_recv,
 ):
     nf, nd, nr, nc = buf.shape
     chunks = nf // chunk
@@ -110,10 +111,6 @@
     def bring(c):
         part = pl.ds(c * chunk, chunk)
         return pltpu.make_async_copy(act.at[part], buf.at[part], in_sem.at[c])
-
-    def put(c):
-        part = pl.ds(c * chunk, chunk)
-        return pltpu.make_async_copy(buf.at[part], a2.at[part], out_sem.at[c])
 
     def remote(src, dst, send, recv, where):
         return pltpu.make_async_remote_copy(
@@ -255,7 +252,7 @@
             u_dy = 0.5 * (u_east[c] - u_west[c])
             v_dy = 0.5 * (v_east[c] - v_west[c])
             for d in range(nd + 1):
-                k_ref[(d, *at)] = face[0, d] * (u_dx - v_dy) + face[1, d] * u_dy - face[2, d] * v_dx
+                k_ref[(d, *at)] = table[mine, 2, d] * (u_dx - v_dy) + table[mine, 3, d] * u_dy - table[mine, 4, d] * v_dx
 
     def mean(x, y):
         return [0.5 * (p + q) for p, q in zip(x, y)]
@@ -289,8 +286,8 @@
         ]
 
     def edges(f):
-        speed_x = [gs[f] * t for t in split_cols(cosb[...])]
-        speed_y = [gs[f] * t for t in split_cols(sinb[...])]
+        speed_x = [gs[f] * t for t in split_cols(wave[mine, 0])]
+        speed_y = [gs[f] * t for t in split_cols(wave[mine, 1])]
         lands = [load_row(rows, 11 + i) for i in range(7)]
 
         def cells(ref, w, i):
@@ -314,7 +311,7 @@
                 border[i, :, pl.ds(c * LANES, LANES)] = tiles[c]
 
     def one(f, d):
-        speed_x, speed_y = gs[f] * trig[0, d], gs[f] * trig[1, d]
+        speed_x, speed_y = gs[f] * table[mine, 0, d], gs[f] * table[mine, 1, d]
         lands = load_tiles(sea)
         cx = [[speed_x + t for t in row] for row in load_tiles(ub)]
         cy = [[speed_y + t for t in row] for row in load_tiles(vb)]
@@ -363,112 +360,211 @@
             return 0
 
         lax.fori_loop(0, chunk, work, 0)
-        put(c).start()
         for side in range(sides):
             turn(side, c).start()
+
+        @pl.when(c > 0)
+        def _():
+            refract_chunk(c - 1)
+
         return 0
 
-    lax.fori_loop(0, chunks, work_chunk, 0)
-
-    def finish(c, _):
-        put(c).wait()
+    def refract_chunk(c):
         for side in range(sides):
-            turn(side, c).wait()
-
-        @pl.when(has_prev)
-        def _():
-            up(c).wait_send()
-
-        @pl.when(has_next)
-        def _():
-            down(c).wait_send()
-
-        return 0
-
-    lax.fori_loop(0, chunks, finish, 0)
-
-    @pl.when(has_prev)
-    def _():
-        cur_up().wait_send()
-        land_up().wait_send()
-
-    @pl.when(has_next)
-    def _():
-        cur_down().wait_send()
-        land_down().wait_send()
-
-
-def refract_kernel(a2, got, k_ref, table, weight, new, stress):
-    nf, nd, nr, nc = a2.shape
-    step = pl.program_id(0)
-
-    @pl.when(step == 0)
-    def _():
-        stress[...] = jnp.zeros(stress.shape, F32)
-
-    def work(i, _):
-        f = step * nf + i
-        for r in range(nr // SUBS):
-            for c in range(nc // LANES):
-                at = (pl.ds(r * SUBS, SUBS), pl.ds(c * LANES, LANES))
-                here = a2[(i, 0, *at)]
-                flux = pick(k_ref[(0, *at)], got[(0, i, *at)], here)
+            turn(side, c).wait_recv()
+
+        def work(i, _):
+            refract(c * chunk + i)
+            return 0
+
+        lax.fori_loop(0, chunk, work, 0)
+
+    def refract(f):
+        for r in range(rt):
+            for q in range(ct):
+                at = (pl.ds(r * SUBS, SUBS), pl.ds(q * LANES, LANES))
+                here = buf[(f, 0, *at)]
+                flux = pick(k_ref[(0, *at)], got[(0, f, *at)], here)
                 total = even = odd = None
                 for d in range(nd):
-                    ahead = a2[(i, d + 1, *at)] if d + 1 < nd else got[(got.shape[0] - 1, i, *at)]
-                    after = pick(k_ref[(d + 1, *at)], here, ahead)
-                    value = here - (after - flux)
-                    new[(i, d, *at)] = value
-                    p, q = table[0, d] * value, table[1, d] * value
+                    ahead = buf[(f, d + 1, *at)] if d + 1 < nd else got[(sides - 1, f, *at)]
+                    after_d = pick(k_ref[(d + 1, *at)], here, ahead)
+                    value = here - (after_d - flux)
+                    buf[(f, d, *at)] = value
+                    x, y = table[mine, 5, d] * value, table[mine, 6, d] * value
                     total = value if d == 0 else total + value
-                    even = p if d == 0 else even + p
-                    odd = q if d == 0 else odd + q
-                    here, flux = ahead, after
+                    even = x if d == 0 else even + x
+                    odd = y if d == 0 else odd + y
+                    here, flux = ahead, after_d
                 w, wr = weight[0, f], weight[1, f]
                 half = (0.5 * w) * total
                 stress[(0, *at)] += wr * (total + even) - half
                 stress[(1, *at)] += wr * odd
                 stress[(2, *at)] += wr * ((total + total) - even) - half
+
+    stress[...] = jnp.zeros(stress.shape, F32)
+    lax.fori_loop(0, chunks, work_chunk, 0)
+    refract_chunk(chunks - 1)
+
+    def finish(c, _):
+        for side in range(sides):
+            turn(side, c).wait_send()
+
+        @pl.when(has_prev)
+        def _():
+            up(c).wait_send()
+
+        @pl.when(has_next)
+        def _():
+            down(c).wait_send()
+
         return 0
 
-    lax.fori_loop(0, nf, work, 0)
-
-
-def with_rows(value, axis):
-    count, length = lax.axis_size(axis), value.shape[1]
-    up = [(i, i + 1) for i in range(count - 1)]
-    before = lax.ppermute(value[:, length - 1:], axis, up)
-    after = lax.ppermute(value[:, :1], axis, [(j, i) for i, j in up])
-    return jnp.concatenate([before, value, after], axis=1)
-
-
-def col_slope(values):
-    padded = jnp.pad(values[1:-1], ((0, 0), (1, 1)))
-    return 0.5 * (padded[:, 2:] - padded[:, :-2])
-
-
-def row_slope(values):
-    return 0.5 * (values[2:] - values[:-2])
+    lax.fori_loop(0, chunks, finish, 0)
+
+    @pl.when(has_prev)
+    def _():
+        cur_up().wait_send()
+        land_up().wait_send()
+
+    @pl.when(has_next)
+    def _():
+        cur_down().wait_send()
+        land_down().wait_send()
+
+
+def force_kernel(n_pts, n_dir, stress, force, full, top, bot, send, recv):
+    nr = stress.shape[1]
+    me = lax.axis_index("pts")
+    mine = lax.axis_index("dir")
+    has_prev = me > 0
+    has_next = me < n_pts - 1
+    before = jnp.maximum(me - 1, 0)
+    after = jnp.minimum(me + 1, n_pts - 1)
+    barrier = pltpu.get_barrier_semaphore()
+    sectors = [lax.rem(mine + j, n_dir) for j in range(n_dir)]
+
+    def greet(point, sector):
+        pl.semaphore_signal(
+            barrier, inc=1, device_id={"pts": point, "dir": sector}, device_id_type=MESH
+        )
+
+    for sector in sectors[1:]:
+        greet(me, sector)
+
+    @pl.when(has_prev)
+    def _():
+        for sector in sectors:
+            greet(before, sector)
+
+    @pl.when(has_next)
+    def _():
+        for sector in sectors:
+            greet(after, sector)
+
+    @pl.when(jnp.logical_not(has_prev))
+    def _():
+        top[...] = jnp.zeros(top.shape, F32)
+
+    @pl.when(jnp.logical_not(has_next))
+    def _():
+        bot[...] = jnp.zeros(bot.shape, F32)
+
+    full[mine] = stress[...]
+    others = has_prev.astype(jnp.int32) + has_next.astype(jnp.int32)
+    pl.semaphore_wait(barrier, n_dir * others + n_dir - 1)
+
+    def copy(kind, j, slot):
+        src = (
+            stress, stress.at[:, pl.ds(nr - SUBS, SUBS)], stress.at[:, pl.ds(0, SUBS)]
+        )[kind]
+        dst = (full, top, bot)[kind].at[slot]
+        return pltpu.make_async_remote_copy(
+            src_ref=src, dst_ref=dst, send_sem=send.at[kind, j], recv_sem=recv.at[kind, slot],
+            device_id={"pts": (me, after, before)[kind], "dir": sectors[j]}, device_id_type=MESH,
+        )
+
+    @pl.when(has_next)
+    def _():
+        for j in range(n_dir):
+            copy(1, j, mine).start()
+
+    @pl.when(has_prev)
+    def _():
+        for j in range(n_dir):
+            copy(2, j, mine).start()
+
+    for j in range(1, n_dir):
+        copy(0, j, mine).start()
+    for j in range(1, n_dir):
+        copy(0, j, sectors[j]).wait_recv()
+
+    @pl.when(has_prev)
+    def _():
+        for j in range(n_dir):
+            copy(1, j, sectors[j]).wait_recv()
+
+    @pl.when(has_next)
+    def _():
+        for j in range(n_dir):
+            copy(2, j, sectors[j]).wait_recv()
+
+    def added(load):
+        parts = [load(s) for s in range(n_dir)]
+        total = parts[0]
+        for part in parts[1:]:
+            total = jax.tree.map(jnp.add, total, part)
+        return total
+
+    whole = [added(lambda s: load_tiles(full, s, q)) for q in range(3)]
+    above = [added(lambda s: load_row(top, s, q, SUBS - 1)) for q in range(3)]
+    below = [added(lambda s: load_row(bot, s, q, 0)) for q in range(3)]
+    for out in range(2):
+        ahead, behind = next_row(whole[out], below[out]), prev_row(whole[out], above[out])
+        for r, row in enumerate(whole[out + 1]):
+            east, west = next_col(row), prev_col(row, 0.0)
+            for c in range(len(row)):
+                force[out, pl.ds(r * SUBS, SUBS), pl.ds(c * LANES, LANES)] = -(
+                    0.5 * (ahead[r][c] - behind[r][c]) + 0.5 * (east[c] - west[c])
+                )
+
+    for j in range(1, n_dir):
+        copy(0, j, mine).wait_send()
+
+    @pl.when(has_next)
+    def _():
+        for j in range(n_dir):
+            copy(1, j, mine).wait_send()
+
+    @pl.when(has_prev)
+    def _():
+        for j in range(n_dir):
+            copy(2, j, mine).wait_send()
+
+
+def geometry(n_dir, nd):
+    total = n_dir * nd
+    step = 2.0 * math.pi / total
+    out = np.zeros((n_dir, 7, nd + 1), np.float32)
+    for s in range(n_dir):
+        angle = (s * nd + np.arange(nd)) * step
+        index = np.arange(nd + 1) % nd if n_dir == 2 else s * nd + np.arange(nd + 1)
+        phi = (index - 0.5) * step
+        scale = total / (2.0 * math.pi)
+        cos, sin = np.cos(angle), np.sin(angle)
+        out[s, 0, :nd], out[s, 1, :nd] = cos, sin
+        out[s, 2] = scale * np.sin(phi) * np.cos(phi)
+        out[s, 3] = scale * np.sin(phi) ** 2
+        out[s, 4] = scale * np.cos(phi) ** 2
+        out[s, 5, :nd], out[s, 6, :nd] = cos * cos, sin * cos
+    return out
 
 
 def per_device(action, currents, land_mask, group_speed, group_ratio, bin_weight):
     nf, nd, nr, nc = action.shape
     n_pts, n_dir = lax.axis_size("pts"), lax.axis_size("dir")
-    total_dirs = nd * n_dir
-    step_angle = 2.0 * math.pi / total_dirs
-    offset = lax.axis_index("dir") * nd
-    angles = (offset + jnp.arange(nd)).astype(F32) * step_angle
-    trig = jnp.stack([jnp.cos(angles), jnp.sin(angles)])
-    face_offset = 0 if n_dir == 2 else offset
-    face_index = jnp.arange(nd + 1)
-    if n_dir == 2:
-        face_index = face_index % nd
-    face_angles = ((face_offset + face_index).astype(F32) - 0.5) * step_angle
-    scale = total_dirs / (2.0 * math.pi)
-    fs, fc = jnp.sin(face_angles), jnp.cos(face_angles)
-    face = scale * jnp.stack([fs * fc, fs * fs, fc * fc])
-    cosb = jnp.broadcast_to(trig[0][:, None], (nd, nc))
-    sinb = jnp.broadcast_to(trig[1][:, None], (nd, nc))
+    table = geometry(n_dir, nd)
+    wave = np.ascontiguousarray(np.broadcast_to(table[:, :2, :nd, None], (n_dir, 2, nd, nc)))
     chunk = max(c for c in range(1, 6) if nf % c == 0)
     chunks = nf // chunk
     sides = 1 if n_dir == 2 else 2
@@ -477,56 +573,48 @@
     hbm = pl.BlockSpec(memory_space=pl.ANY)
     dma = pltpu.SemaphoreType.DMA
     halo = pltpu.VMEM((nf, 2, nd, nc), F32)
-    a2, got, turning = pl.pallas_call(
+    weight = jnp.stack([bin_weight, bin_weight * group_ratio])
+    new_action, stress = pl.pallas_call(
         functools.partial(transport_kernel, n_pts, n_dir, chunk),
         out_shape=(
             jax.ShapeDtypeStruct(action.shape, F32),
-            jax.ShapeDtypeStruct((sides, nf, nr, nc), F32),
-            jax.ShapeDtypeStruct((nd + 1, nr, nc), F32),
+            jax.ShapeDtypeStruct((3, nr, nc), F32),
         ),
-        in_specs=[hbm, vmem, vmem, smem, smem, vmem, vmem, smem],
-        out_specs=(hbm, hbm, vmem),
+        in_specs=[hbm, vmem, vmem, smem, smem, smem, vmem],
+        out_specs=(vmem, vmem),
         scratch_shapes=[
-            pltpu.VMEM(action.shape, F32), halo, halo, halo, halo,
+            pltpu.VMEM((sides, nf, nr, nc), F32), pltpu.VMEM((nd + 1, nr, nc), F32),
+            halo, halo, halo, halo,
             pltpu.VMEM((2, SUBS, nc), F32), pltpu.VMEM((2, SUBS, nc), F32),
             pltpu.VMEM((SUBS, nc), jnp.int32), pltpu.VMEM((SUBS, nc), jnp.int32),
             pltpu.VMEM((nr, nc), F32), pltpu.VMEM((nr, nc), F32), pltpu.VMEM((nr, nc), F32),
             pltpu.VMEM((24, nc), F32), pltpu.VMEM((4, nd, nc), F32),
             pltpu.VMEM((sides, nf, nr, nc), F32),
-            dma((chunks,)), dma((chunks,)), dma((chunks,)), dma((chunks,)), dma((chunks,)),
+            dma((chunks,)), dma((chunks,)), dma((chunks,)), dma((chunks,)),
             dma((chunks,)), dma((8,)), dma((sides, chunks)), dma((sides, chunks)),
         ],
         compiler_params=pltpu.CompilerParams(
-            collective_id=0, has_side_effects=True, vmem_limit_bytes=40 * 2**20
+            collective_id=0, has_side_effects=True, vmem_limit_bytes=32 * 2**20
         ),
         name="transport",
-    )(action, currents, land_mask, group_speed, trig, cosb, sinb, face)
-    table = jnp.stack([trig[0] * trig[0], trig[0] * trig[1]])
-    weight = jnp.stack([bin_weight, bin_weight * group_ratio])
-    new_action, stress = pl.pallas_call(
-        refract_kernel,
-        grid=(chunks,),
-        out_shape=(
-            jax.ShapeDtypeStruct(action.shape, F32),
-            jax.ShapeDtypeStruct((3, nr, nc), F32),
+    )(action, currents, land_mask, group_speed, weight, table, wave)
+    force = pl.pallas_call(
+        functools.partial(force_kernel, n_pts, n_dir),
+        out_shape=jax.ShapeDtypeStruct((2, nr, nc), F32),
+        in_specs=[vmem],
+        out_specs=vmem,
+        scratch_shapes=[
+            pltpu.VMEM((n_dir, 3, nr, nc), F32),
+            pltpu.VMEM((n_dir, 3, SUBS, nc), F32), pltpu.VMEM((n_dir, 3, SUBS, nc), F32),
+            dma((3, n_dir)), dma((3, n_dir)),
+        ],
+        compiler_params=pltpu.CompilerParams(
+            collective_id=1, has_side_effects=True, vmem_limit_bytes=16 * 2**20
         ),
-        in_specs=[
-            pl.BlockSpec((chunk, nd, nr, nc), lambda i: (i, 0, 0, 0)),
-            pl.BlockSpec((sides, chunk, nr, nc), lambda i: (0, i, 0, 0)),
-            pl.BlockSpec((nd + 1, nr, nc), lambda i: (0, 0, 0)),
-            smem, smem,
-        ],
-        out_specs=(
-            pl.BlockSpec((chunk, nd, nr, nc), lambda i: (i, 0, 0, 0)),
-            pl.BlockSpec((3, nr, nc), lambda i: (0, 0, 0)),
-        ),
-        compiler_params=pltpu.CompilerParams(vmem_limit_bytes=40 * 2**20),
-        name="refract",
-    )(a2, got, turning, table, weight)
-    ext = lax.psum(with_rows(stress, "pts"), "dir")
-    first = -(row_slope(ext[0]) + col_slope(ext[1]))
-    second = -(row_slope(ext[1]) + col_slope(ext[2]))
-    return new_action, jnp.stack([first, second])
+        cost_estimate=pl.CostEstimate(flops=10**6, bytes_accessed=2 * 10**7, transcendentals=0),
+        name="force",
+    )(stress)
+    return new_action, force
 
 
 def solution(mesh):

time: 101 us -> 95.4 us (0.945)
  waiting for transfers between devices: 19.9 us -> 0 us
  Pallas kernels: 54.7 us -> 71.4 us
  local copies, waits for them, and re-layouts: 12 us -> 21.4 us
  blocking collectives: 7.83 us -> 0 us
  starting transfers between devices: 3.33 us -> 0 us
    ppermute x2 -> x0, waiting for transfers between devices: 19.9 us -> none  [the longest x1 19.9 us: with_rows(): after = lax.ppermute(value[:, :1], axis, [(j, i) for i, j in up])]
    pallas_call x1, Pallas kernels: 9.23 us -> 21 us  [per_device(): pl.pallas_call(functools.partial(force_kernel, n_pts, n_dir), out_shape=j...]
    unnamed x10 -> x14, local copies, waits for them, and re-layouts: 11.8 us -> 21.4 us
    psum x1 -> x0, blocking collectives: 7.83 us -> none  [per_device(): ext = lax.psum(with_rows(stress, 'pts'), 'dir')]
    pallas_call x1, Pallas kernels: 45.5 us -> 50.4 us  [per_device(): pl.pallas_call(functools.partial(transport_kernel, n_pts, n_dir, chunk),...]
    ppermute x2 -> x0, starting transfers between devices: 3.33 us -> none  [the longest x1 2.04 us: with_rows(): before = lax.ppermute(value[:, length - 1:], axis, up)]
  transfers between devices with their start and end apart: 2 -> 0, of which waited for: 1 -> 0; matrix products, arithmetic and copies ran while one was open for 0% -> 0% of each run, Pallas kernels for 0% -> 0%
where the time goes in v1:
time: 95.4 us; the launch traced here: 94.8 us
  Pallas kernels  71.4 us (75%)
  local copies, waits for them, and re-layouts  21.4 us (22%)
  other arithmetic  1.34 us (1%)
    pallas_call x1, Pallas kernels, per_device(): pl.pallas_call(functools.partial(transport_kernel, n_pts, n_dir, chunk),...  50.4 us
    unnamed x14, local copies, waits for them, and re-layouts  21.4 us
    pallas_call x1, Pallas kernels, per_device(): pl.pallas_call(functools.partial(force_kernel, n_pts, n_dir), out_shape=j...  21 us

profile of v1, /device:TPU:0, one launch (start us, length us, event | category | flops | bytes accessed | tf_op | source)
XLA Modules:
  0.0 94.8 jit_solution(3591585652846483283)
XLA Ops:
  0.6 0.7 multiply_bitcast_fusion
  1.3 0.7 pad_maximum_fusion.weight
  2.0 0.0 copy-start.1
  2.0 0.8 copy-done.1
  2.8 0.0 copy-start.2
  2.8 0.8 copy-done.2
  3.6 0.0 copy-start.3
  3.6 0.7 copy-done.3
  4.3 0.0 copy-start.4
  4.3 0.7 copy-done.4
  5.0 0.0 copy-start.5
  5.0 0.7 copy-done.5
  5.6 50.4 %transport.1 = (f32[50,16,16,256]{3,2,1,0:T(8,128)S(1)}, f32[3,16,256]{2,1,0:T(8,128)S(1)}) custom-call(f32[50,16,16,256]{3,2,1,0:T(8,128)} %act.1, f32[2,16,256]{2,1,0:T(8,128)S(1)} %copy-done.2, s32[16,256]{1,0:T(8,128)S(1)} %copy-done.3, f32[50]{0:T(128)S(1)} %copy-done.5, f32[2,50]{1,0:T(2,128)S(1)} %pad_maximum_fusion.weight, ...), custom_call_target="tpu_custom_call" | custom-call | tf_op jit(solution)/shard_map/transport/pallas_call | solution.py:577
  56.1 0.0 copy-start
  56.1 4.7 %copy-done = f32[50,16,16,256]{3,2,1,0:T(8,128)} copy-done((f32[50,16,16,256]{3,2,1,0:T(8,128)}, f32[50,16,16,256]{3,2,1,0:T(8,128)S(1)}, u32[]{:S(2)}) %copy-start) | copy-done | bytes 13107224
  60.7 21.0 %force.1 = f32[2,16,256]{2,1,0:T(8,128)S(1)} custom-call(f32[3,16,256]{2,1,0:T(8,128)S(1)} %get-tuple-element.5.stress), custom_call_target="tpu_custom_call" | custom-call | flops 1000000 | bytes 20000000 | tf_op jit(solution)/shard_map/force/pallas_call | solution.py:601
  81.7 12.5 %copy.12 = f32[50,16,16,256]{3,2,1,0:T(8,128)} copy(f32[50,16,16,256]{3,2,1,0:T(8,128)} %copy-done) | data formatting | bytes 26214400
  94.2 0.6 copy.13
Async XLA Ops:
  2.0 0.8 copy-start.1
  2.8 0.8 copy-start.2
  3.6 0.7 copy-start.3
  4.3 0.7 copy-start.4
  5.0 0.7 copy-start.5
  56.1 4.7 %copy-start = (f32[50,16,16,256]{3,2,1,0:T(8,128)}, f32[50,16,16,256]{3,2,1,0:T(8,128)S(1)}, u32[]{:S(2)}) copy-start(f32[50,16,16,256]{3,2,1,0:T(8,128)S(1)} %get-tuple-element.8) | copy-start | bytes 39321604

commit v2 on v1

--- a/solution.py
+++ b/solution.py
@@ -90,11 +90,11 @@
 
 def transport_kernel(
     n_pts, n_dir, chunk,
-    act, cur, land, gs, weight, table, wave,
-    buf, stress,
-    got, k_ref, own_top, own_bot, halo_top, halo_bot, cur_top, cur_bot, land_top, land_bot,
+    act, cur_in, land_in, wave_in, gs, table,
+    a2, got, k_out,
+    buf, cur, land, wave, k_ref, own_top, own_bot, halo_top, halo_bot, cur_top, cur_bot, land_top, land_bot,
     ub, vb, sea, rows, border, sel,
-    in_sem, up_send, up_recv, down_send, down_recv, cur_sem, dir_send, dir_recv,
+    in_sem, out_sem, small_sem, up_send, up_recv, down_send, down_recv, cur_sem, dir_send, dir_recv,
 ):
     nf, nd, nr, nc = buf.shape
     chunks = nf // chunk
@@ -112,6 +112,16 @@
         part = pl.ds(c * chunk, chunk)
         return pltpu.make_async_copy(act.at[part], buf.at[part], in_sem.at[c])
 
+    def put(c):
+        part = pl.ds(c * chunk, chunk)
+        return pltpu.make_async_copy(buf.at[part], a2.at[part], out_sem.at[c])
+
+    small = [
+        pltpu.make_async_copy(src, dst, small_sem.at[i])
+        for i, (src, dst) in enumerate(((cur_in, cur), (land_in, land), (wave_in, wave)))
+    ]
+    put_turning = pltpu.make_async_copy(k_ref, k_out, small_sem.at[3])
+
     def remote(src, dst, send, recv, where):
         return pltpu.make_async_remote_copy(
             src_ref=src, dst_ref=dst, send_sem=send, recv_sem=recv,
@@ -147,6 +157,9 @@
 
     sides = sel.shape[0]
 
+    for one_copy in small:
+        one_copy.start()
+
     def start_in(c, _):
         bring(c).start()
         return 0
@@ -187,6 +200,9 @@
 
     others = has_prev.astype(jnp.int32) + has_next.astype(jnp.int32)
     pl.semaphore_wait(barrier, others + (2 if n_dir > 2 else 1))
+
+    for one_copy in small:
+        one_copy.wait()
 
     @pl.when(has_prev)
     def _():
@@ -363,74 +379,77 @@
         for side in range(sides):
             turn(side, c).start()
 
-        @pl.when(c > 0)
+        put(c).start()
+        return 0
+
+    put_turning.start()
+    lax.fori_loop(0, chunks, work_chunk, 0)
+    put_turning.wait()
+
+    def finish(c, _):
+        for side in range(sides):
+            turn(side, c).wait()
+        put(c).wait()
+
+        @pl.when(has_prev)
         def _():
-            refract_chunk(c - 1)
+            up(c).wait_send()
+
+        @pl.when(has_next)
+        def _():
+            down(c).wait_send()
 
         return 0
 
-    def refract_chunk(c):
-        for side in range(sides):
-            turn(side, c).wait_recv()
-
-        def work(i, _):
-            refract(c * chunk + i)
-            return 0
-
-        lax.fori_loop(0, chunk, work, 0)
-
-    def refract(f):
-        for r in range(rt):
-            for q in range(ct):
-                at = (pl.ds(r * SUBS, SUBS), pl.ds(q * LANES, LANES))
-                here = buf[(f, 0, *at)]
-                flux = pick(k_ref[(0, *at)], got[(0, f, *at)], here)
+    lax.fori_loop(0, chunks, finish, 0)
+
+    @pl.when(has_prev)
+    def _():
+        cur_up().wait_send()
+        land_up().wait_send()
+
+    @pl.when(has_next)
+    def _():
+        cur_down().wait_send()
+        land_down().wait_send()
+
+
+def refract_kernel(a2, got, k_ref, table, wt, ratio, new, stress):
+    nf, nd, nr, nc = a2.shape
+    step = pl.program_id(0)
+    mine = lax.axis_index("dir")
+
+    @pl.when(step == 0)
+    def _():
+        stress[...] = jnp.zeros(stress.shape, F32)
+
+    def work(i, _):
+        f = step * nf + i
+        for r in range(nr // SUBS):
+            for c in range(nc // LANES):
+                at = (pl.ds(r * SUBS, SUBS), pl.ds(c * LANES, LANES))
+                here = a2[(i, 0, *at)]
+                flux = pick(k_ref[(0, *at)], got[(0, i, *at)], here)
                 total = even = odd = None
                 for d in range(nd):
-                    ahead = buf[(f, d + 1, *at)] if d + 1 < nd else got[(sides - 1, f, *at)]
-                    after_d = pick(k_ref[(d + 1, *at)], here, ahead)
-                    value = here - (after_d - flux)
-                    buf[(f, d, *at)] = value
-                    x, y = table[mine, 5, d] * value, table[mine, 6, d] * value
+                    ahead = a2[(i, d + 1, *at)] if d + 1 < nd else got[(got.shape[0] - 1, i, *at)]
+                    after = pick(k_ref[(d + 1, *at)], here, ahead)
+                    value = here - (after - flux)
+                    new[(i, d, *at)] = value
+                    p, q = table[mine, 5, d] * value, table[mine, 6, d] * value
                     total = value if d == 0 else total + value
-                    even = x if d == 0 else even + x
-                    odd = y if d == 0 else odd + y
-                    here, flux = ahead, after_d
-                w, wr = weight[0, f], weight[1, f]
+                    even = p if d == 0 else even + p
+                    odd = q if d == 0 else odd + q
+                    here, flux = ahead, after
+                w = wt[f]
+                wr = w * ratio[f]
                 half = (0.5 * w) * total
                 stress[(0, *at)] += wr * (total + even) - half
                 stress[(1, *at)] += wr * odd
                 stress[(2, *at)] += wr * ((total + total) - even) - half
-
-    stress[...] = jnp.zeros(stress.shape, F32)
-    lax.fori_loop(0, chunks, work_chunk, 0)
-    refract_chunk(chunks - 1)
-
-    def finish(c, _):
-        for side in range(sides):
-            turn(side, c).wait_send()
-
-        @pl.when(has_prev)
-        def _():
-            up(c).wait_send()
-
-        @pl.when(has_next)
-        def _():
-            down(c).wait_send()
-
         return 0
 
-    lax.fori_loop(0, chunks, finish, 0)
-
-    @pl.when(has_prev)
-    def _():
-        cur_up().wait_send()
-        land_up().wait_send()
-
-    @pl.when(has_next)
-    def _():
-        cur_down().wait_send()
-        land_down().wait_send()
+    lax.fori_loop(0, nf, work, 0)
 
 
 def force_kernel(n_pts, n_dir, stress, force, full, top, bot, send, recv):
@@ -565,39 +584,63 @@
     n_pts, n_dir = lax.axis_size("pts"), lax.axis_size("dir")
     table = geometry(n_dir, nd)
     wave = np.ascontiguousarray(np.broadcast_to(table[:, :2, :nd, None], (n_dir, 2, nd, nc)))
-    chunk = max(c for c in range(1, 6) if nf % c == 0)
+    chunk = max(c for c in (1, 2) if nf % c == 0)
     chunks = nf // chunk
+    block = max(c for c in range(1, 6) if nf % c == 0)
     sides = 1 if n_dir == 2 else 2
     vmem = pl.BlockSpec(memory_space=pltpu.VMEM)
     smem = pl.BlockSpec(memory_space=pltpu.SMEM)
     hbm = pl.BlockSpec(memory_space=pl.ANY)
     dma = pltpu.SemaphoreType.DMA
     halo = pltpu.VMEM((nf, 2, nd, nc), F32)
-    weight = jnp.stack([bin_weight, bin_weight * group_ratio])
-    new_action, stress = pl.pallas_call(
+    a2, got, turning = pl.pallas_call(
         functools.partial(transport_kernel, n_pts, n_dir, chunk),
         out_shape=(
             jax.ShapeDtypeStruct(action.shape, F32),
-            jax.ShapeDtypeStruct((3, nr, nc), F32),
+            jax.ShapeDtypeStruct((sides, nf, nr, nc), F32),
+            jax.ShapeDtypeStruct((nd + 1, nr, nc), F32),
         ),
-        in_specs=[hbm, vmem, vmem, smem, smem, smem, vmem],
-        out_specs=(vmem, vmem),
+        in_specs=[hbm, hbm, hbm, hbm, smem, smem],
+        out_specs=(hbm, hbm, hbm),
         scratch_shapes=[
-            pltpu.VMEM((sides, nf, nr, nc), F32), pltpu.VMEM((nd + 1, nr, nc), F32),
+            pltpu.VMEM(action.shape, F32), pltpu.VMEM(currents.shape, F32),
+            pltpu.VMEM(land_mask.shape, jnp.int32), pltpu.VMEM(wave.shape, F32),
+            pltpu.VMEM((nd + 1, nr, nc), F32),
             halo, halo, halo, halo,
             pltpu.VMEM((2, SUBS, nc), F32), pltpu.VMEM((2, SUBS, nc), F32),
             pltpu.VMEM((SUBS, nc), jnp.int32), pltpu.VMEM((SUBS, nc), jnp.int32),
             pltpu.VMEM((nr, nc), F32), pltpu.VMEM((nr, nc), F32), pltpu.VMEM((nr, nc), F32),
             pltpu.VMEM((24, nc), F32), pltpu.VMEM((4, nd, nc), F32),
             pltpu.VMEM((sides, nf, nr, nc), F32),
-            dma((chunks,)), dma((chunks,)), dma((chunks,)), dma((chunks,)),
+            dma((chunks,)), dma((chunks,)), dma((4,)),
+            dma((chunks,)), dma((chunks,)), dma((chunks,)),
             dma((chunks,)), dma((8,)), dma((sides, chunks)), dma((sides, chunks)),
         ],
         compiler_params=pltpu.CompilerParams(
-            collective_id=0, has_side_effects=True, vmem_limit_bytes=32 * 2**20
+            collective_id=0, has_side_effects=True, vmem_limit_bytes=60 * 2**20
         ),
         name="transport",
-    )(action, currents, land_mask, group_speed, weight, table, wave)
+    )(action, currents, land_mask, wave, group_speed, table)
+    new_action, stress = pl.pallas_call(
+        refract_kernel,
+        grid=(nf // block,),
+        out_shape=(
+            jax.ShapeDtypeStruct(action.shape, F32),
+            jax.ShapeDtypeStruct((3, nr, nc), F32),
+        ),
+        in_specs=[
+            pl.BlockSpec((block, nd, nr, nc), lambda i: (i, 0, 0, 0)),
+            pl.BlockSpec((sides, block, nr, nc), lambda i: (0, i, 0, 0)),
+            pl.BlockSpec((nd + 1, nr, nc), lambda i: (0, 0, 0)),
+            smem, smem, smem,
+        ],
+        out_specs=(
+            pl.BlockSpec((block, nd, nr, nc), lambda i: (i, 0, 0, 0)),
+            pl.BlockSpec((3, nr, nc), lambda i: (0, 0, 0)),
+        ),
+        compiler_params=pltpu.CompilerParams(vmem_limit_bytes=60 * 2**20),
+        name="refract",
+    )(a2, got, turning, table, bin_weight, group_ratio)
     force = pl.pallas_call(
         functools.partial(force_kernel, n_pts, n_dir),
         out_shape=jax.ShapeDtypeStruct((2, nr, nc), F32),

time: 95.4 us -> 83.7 us (0.88)
  local copies, waits for them, and re-layouts: 21.4 us -> 1.41 us
  Pallas kernels: 71.4 us -> 80.7 us
  other arithmetic: 1.34 us -> 0 us
    unnamed x14 -> x3, local copies, waits for them, and re-layouts: 21.4 us -> 1.41 us
    pallas_call x0 -> x1, Pallas kernels: none -> 15.4 us  [per_device(): pl.pallas_call(refract_kernel, grid=(nf // block,), out_shape=(jax.ShapeD...]
    pallas_call x1, Pallas kernels: 50.4 us -> 44.7 us  [per_device(): pl.pallas_call(functools.partial(transport_kernel, n_pts, n_dir, chunk),...]
    another operation x2 -> x0, other arithmetic: 1.34 us -> none  [per_device(): weight = jnp.stack([bin_weight, bin_weight * group_ratio])]
where the time goes in v2:
time: 83.7 us; the launch traced here: 82.8 us
  Pallas kernels  80.7 us (96%)
  local copies, waits for them, and re-layouts  1.41 us (2%)
    pallas_call x1, Pallas kernels, per_device(): pl.pallas_call(functools.partial(transport_kernel, n_pts, n_dir, chunk),...  44.7 us
    pallas_call x1, Pallas kernels, per_device(): pl.pallas_call(functools.partial(force_kernel, n_pts, n_dir), out_shape=j...  20.6 us
    pallas_call x1, Pallas kernels, per_device(): pl.pallas_call(refract_kernel, grid=(nf // block,), out_shape=(jax.ShapeD...  15.4 us

profile of v2, /device:TPU:0, one launch (start us, length us, event | category | flops | bytes accessed | tf_op | source)
XLA Modules:
  0.0 82.8 jit_solution(15327167062527466955)
XLA Ops:
  0.6 44.7 %transport.1 = (f32[50,16,16,256]{3,2,1,0:T(8,128)}, f32[1,50,16,256]{3,2,1,0:T(8,128)}, f32[17,16,256]{2,1,0:T(8,128)}) custom-call(f32[50,16,16,256]{3,2,1,0:T(8,128)} %act.1, f32[2,16,256]{2,1,0:T(8,128)} %cur_in.1, s32[16,256]{1,0:T(8,128)} %land_in.1, f32[2,2,16,256]{3,2,1,0:T(8,128)} %constant.4.clone.wave_in, f32[50]{0:T(128)} %gs.1, ...), custom_call_target="tpu_custom_call" | custom-call | tf_op jit(solution)/shard_map/transport/pallas_call | solution.py:596
  45.3 15.4 %refract.1 = (f32[50,16,16,256]{3,2,1,0:T(8,128)}, f32[3,16,256]{2,1,0:T(8,128)}) custom-call(f32[50,16,16,256]{3,2,1,0:T(8,128)} %get-tuple-element.7.a2, f32[1,50,16,256]{3,2,1,0:T(8,128)} %get-tuple-element.8.got, f32[17,16,256]{2,1,0:T(8,128)} %get-tuple-element.9.k_ref, f32[2,7,17]{2,1,0:T(8,128)} %constant.5.clone.table, f32[50]{0:T(128)} %wt.1, f32[50]{0:T(128)} %ratio.1), custom_call_target="tpu_custom_call" | custom-call | tf_op jit(solution)/shard_map/refract/pallas_call | solution.py:624
  60.7 0.0 copy-start
  60.7 0.8 copy-done
  61.5 20.6 %force.1 = f32[2,16,256]{2,1,0:T(8,128)S(1)} custom-call(f32[3,16,256]{2,1,0:T(8,128)S(1)} %copy-done), custom_call_target="tpu_custom_call" | custom-call | flops 1000000 | bytes 20000000 | tf_op jit(solution)/shard_map/force/pallas_call | solution.py:644
  82.1 0.6 copy.11
Async XLA Ops:
  60.7 0.8 copy-start
